TPU v7x, 32 devices: a whole 2x2x4 slice. The times are simulated.
32 devices in a mesh: row: 4 (over z), ma: 8 (over y, x, core).
Axes of the slice: x: 2, y: 2, z: 4, core: 2. Of those that a mesh axis runs over, the one named last changes fastest.
Arguments:
- spectra: float32 [4, 2, 128, 4224], P(None, None, 'row', 'ma'), may hold values from -6 to 6
- dtheta_table: bfloat16 [4224, 768], P('ma'), may hold values from -0.046875 to 0.046875
- dphi_table: bfloat16 [4224, 768], P('ma'), may hold values from -0.046875 to 0.046875
- analysis_table: bfloat16 [4224, 768], P('ma'), may hold values from -6 to 6
- pair_index: int32 [8], replicated, may hold values from 0 to 255, as said below
- diffusivity: float32 [4], replicated, may hold values from 0.0001 to 0.0004
Outputs:
- new_spectra: float32 [4, 2, 128, 4224], P(None, None, 'row', 'ma')
Inputs may be any that keep to these rules, and one draw needn't show every extreme that they name: 8 distinct values, among them always both 0 and the largest; position g holds the orders pair_index[g] and 511 - pair_index[g].
All inputs are finite; a program needn't handle non-finite values.
Results may differ from a plain program's by a relative error of at most 0.0057.
Values may be sent and summed in bfloat16 or wider, within the bound.
A program may use at most 64 MiB of HBM per device.

v0:
```python
import functools

import jax
import jax.numpy as jnp
from jax import lax
from jax.experimental import pallas as pl
from jax.experimental.pallas import tpu as pltpu
from jax.sharding import PartitionSpec as P

LMAX = 511
ROTATION = 2.0
SHELL_RADIUS = 16.0
RADII = 8
VMEM_LIMIT = 62 * 1024 * 1024


def slot_rows(lowest, slots):
    slot = lax.broadcasted_iota(jnp.int32, (1, slots), 1)
    first = slot < LMAX + 1 - lowest
    held = slot < LMAX + 2
    second = jnp.logical_and(jnp.logical_not(first), held)
    degree = jnp.where(first, lowest + slot, slot - 1)
    order = jnp.where(first, lowest, LMAX - lowest)
    return first, second, held, degree, order


def greet(axis_sizes):
    barrier = pltpu.get_barrier_semaphore()
    total = 0
    for axis, size in axis_sizes:
        me = lax.axis_index(axis)
        for k in range(1, size):
            pl.semaphore_signal(
                barrier, inc=1, device_id={axis: lax.rem(me + k, size)},
                device_id_type=pl.DeviceIdType.MESH,
            )
        total += size - 1
    pl.semaphore_wait(barrier, total)


def ring(me, n):
    tall = n // 4

    def target(dy, dx, dc):
        y, x, c = me // 4, lax.rem(me // 2, 2), lax.rem(me, 2)
        return lax.rem(y + dy, tall) * 4 + lax.rem(x + dx, 2) * 2 + lax.rem(c + dc, 2)

    return target


def far_first(n):
    steps = [(dy, dx, dc) for dy in range(n // 4) for dx in range(2) for dc in range(2)]
    return sorted(steps[1:], key=lambda d: (-((d[0] > 0) + d[1]), d[2], d[1]))


def step_kernel(
    n, rows_count, partner, pair, diffusivity, spectra_hbm, dtheta_hbm, dphi_hbm, analysis_hbm, out,
    spectra, dtheta, dphi, analysis, send, x, states, sums, got, edges, right, carries,
    load_sem, send_sem, recv_sem, back_send, back_recv, edge_send, edge_recv,
):
    loads = [
        pltpu.make_async_copy(source, target, load_sem.at[i])
        for i, (source, target) in enumerate(
            [(spectra_hbm, spectra), (dtheta_hbm, dtheta), (dphi_hbm, dphi), (analysis_hbm, analysis)]
        )
    ]
    for load in loads:
        load.start()
    greet([("ma", n), ("row", rows_count)])
    me = lax.axis_index("ma")
    row = lax.axis_index("row")
    slots = spectra.shape[3]
    points = spectra.shape[2]
    radii = RADII
    groups = points // radii
    halves = n // groups
    width = dtheta.shape[1] // halves
    chunks = width // 128
    orders = 2 * n
    keep = jnp.where(pair[me] == 0, 0.0, 1.0).astype(jnp.float32)
    lowest = pair[me]
    first, second, held, degree, order = slot_rows(lowest, slots)
    alive = held.astype(jnp.float32)
    l = degree.astype(jnp.float32)
    m = order.astype(jnp.float32)
    lower = jnp.sqrt((l * l - m * m) * alive / jnp.maximum(4.0 * l * l - 1.0, 1.0)) * ROTATION
    u = l + 1.0
    upper = jnp.sqrt(jnp.maximum((u * u - m * m) / (4.0 * u * u - 1.0), 0.0))
    upper = jnp.where(degree < LMAX, upper * alive, 0.0) * ROTATION
    spin = ROTATION * m / (l * (l + 1.0) + 2.0) * alive

    all_points = points * rows_count
    field = lax.broadcasted_iota(jnp.int32, (8, 1), 0) // 2
    nu = jnp.zeros((8, 1), jnp.float32)
    for f in range(4):
        nu = jnp.where(field == f, diffusivity[f], nu)
    off = nu * float((all_points + 1) ** 2)
    half_excess = (1.0 + nu * (l * (l + 1.0) / SHELL_RADIUS**2)) / (2.0 * off)
    root = jnp.sqrt(half_excess * half_excess + 2.0 * half_excess)
    inverse = 1.0 + half_excess + root
    rho = 1.0 / inverse
    log_rho = -jnp.log(inverse)
    inner = 1.0 / (2.0 * off * root)
    at = lax.broadcasted_iota(jnp.int32, (radii, slots), 0)
    near = (at + 1).astype(jnp.float32)
    far = (radii - at).astype(jnp.float32)

    def power(exponent):
        return jnp.exp(log_rho * exponent)

    for load in loads[:3]:
        load.wait()

    def block_for(e):
        group = e // halves
        half = lax.rem(e, halves)
        x = spectra[:, :, pl.ds(pl.multiple_of(group * radii, radii), radii), :]
        x = x.reshape(8 * radii, slots)
        lhs = jnp.concatenate([jnp.where(first, x, 0.0), jnp.where(second, x, 0.0)], axis=0)
        lhs = lhs.astype(jnp.bfloat16)
        columns = pl.ds(pl.multiple_of(half * width, 128), width)
        t = jnp.dot(lhs, dtheta[:, columns], preferred_element_type=jnp.float32)
        d = jnp.dot(lhs, dphi[:, columns], preferred_element_type=jnp.float32)
        t = t.reshape(2, 4, 2, radii, width)
        d = d.reshape(2, 4, 2, radii, width)
        parts = []
        for j in range(2):
            z_t, w_t, s_t, a_t = (t[j, f] for f in range(4))
            z_d, w_d, s_d, a_d = (d[j, f] for f in range(4))
            pieces = [
                (w_t[0] + z_d[1], w_t[1] - z_d[0]),
                (z_t[0] - w_d[1], z_t[1] + w_d[0]),
                (s_t[0], s_t[1]),
                (-s_d[1], s_d[0]),
                (a_d[1], -a_d[0]),
                (a_t[0], a_t[1]),
            ]
            for real, imag in pieces:
                parts += [real, imag * keep if j == 0 else imag]
        return jnp.concatenate(parts, axis=0).astype(jnp.bfloat16)

    def grid_copy(e, source, c):
        return pltpu.make_async_remote_copy(
            src_ref=send.at[c, e], dst_ref=x.at[c, source],
            send_sem=send_sem.at[c, e], recv_sem=recv_sem.at[c, source],
            device_id={"ma": e}, device_id_type=pl.DeviceIdType.MESH,
        )

    def back_copy(e, source, c):
        return pltpu.make_async_remote_copy(
            src_ref=sums.at[c, e], dst_ref=got.at[c, source],
            send_sem=back_send.at[c, e], recv_sem=back_recv.at[c, source],
            device_id={"ma": e}, device_id_type=pl.DeviceIdType.MESH,
        )

    target = ring(me, n)
    for step in far_first(n):
        e = target(*step)
        value = block_for(e)
        for c in range(chunks):
            send[c, e] = value[:, c * 128 : (c + 1) * 128]
        grid_copy(e, me, 0).start()
    for c in range(1, chunks):
        for step in far_first(n):
            grid_copy(target(*step), me, c).start()
    value = block_for(me)
    for c in range(chunks):
        x[c, me] = value[:, c * 128 : (c + 1) * 128]

    def couple(v):
        edge = jnp.zeros((points, 1), jnp.float32)
        below = jnp.concatenate([edge, v[:, : slots - 1]], axis=1)
        above = jnp.concatenate([v[:, 1:], edge], axis=1)
        return lower * below + upper * above

    z0, z1 = (jnp.where(held, spectra[0, c], 0.0) for c in range(2))
    w0, w1 = (jnp.where(held, spectra[1, c], 0.0) for c in range(2))
    right[0, 0] = z0 - spin * z1 + couple(w0) * alive
    right[0, 1] = z1 + spin * z0 + couple(w1) * alive
    right[1, 0] = w0 - spin * w1 - couple(z0) * alive
    right[1, 1] = w1 + spin * w0 - couple(z1) * alive
    for f in (2, 3):
        for c in range(2):
            right[f, c] = jnp.where(held, spectra[f, c], 0.0)

    zero = jnp.zeros((radii, 128), jnp.float32)
    for q in range(12):
        states[3 * orders, q] = zero

    def chunk_step(c, carry):
        def arrive(k, carry):
            e = lax.rem(me + k, n)
            grid_copy(e, e, c).wait_recv()
            return carry

        lax.fori_loop(1, n, arrive, 0)

        def unpack(g, carry):
            block = x[c, g].astype(jnp.float32).reshape(2, 6, 2, radii, 128)
            for j in range(2):
                at_order = 2 * g + j
                u_t, u_p, s_t, s_p, b_t, b_p = (block[j, q] for q in range(6))
                for q, (p, t) in enumerate(((b_p, b_t), (u_p, u_t), (s_p, s_t))):
                    plus = (p[0] - t[1], p[1] + t[0])
                    minus = (p[0] + t[1], p[1] - t[0])
                    parts = (plus[0], plus[1], minus[0], minus[1])
                    turned = (minus[0], -minus[1], plus[0], -plus[1])
                    for i in range(4):
                        states[at_order, 4 * q + i] = parts[i]
                        states[orders + at_order, 4 * q + i] = turned[i]
                        states[2 * orders + at_order, 4 * q + i] = 0.5 * parts[i]
            return carry

        lax.fori_loop(0, n, unpack, 0)

        def one_order(t, carry):
            def add(a, total):
                b = partner[t * orders + a]
                vp, vm, yp, ym, wp, wm = (
                    (states[a, 2 * q], states[a, 2 * q + 1], states[b, 2 * q], states[b, 2 * q + 1])
                    for q in range(6)
                )

                def square(v):
                    ar, ai, br, bi = v
                    return ar * br - ai * bi, ar * bi + ai * br

                def cross(v, w):
                    ar, ai, br, bi = v
                    cr, ci, dr, di = w
                    return (
                        (ar * dr - ai * di) + (cr * br - ci * bi),
                        (ar * di + ai * dr) + (cr * bi + ci * br),
                    )

                terms = []
                for v, y in ((vp, yp), (vm, ym)):
                    first_term, second_term = square(v), square(y)
                    terms += [first_term[0] - second_term[0], first_term[1] - second_term[1]]
                heat, other = cross(ym, wp), cross(yp, wm)
                terms += [heat[0] + other[0], heat[1] + other[1]]
                bent, other = cross(ym, vp), cross(yp, vm)
                terms += [bent[0] - other[0], bent[1] - other[1]]
                return tuple(v + w for v, w in zip(total, terms))

            pr, pi, mr, mi, hr, hi, er, ei = lax.fori_loop(0, orders, add, (zero,) * 8, unroll=8)
            rows = [pi - mi, mr - pr, pr + mr, pi + mi, -hr, -hi, ei, -er]
            rows = (0.5 * jnp.concatenate(rows, axis=0)).astype(jnp.bfloat16)
            sums[c, t // 2, pl.ds(pl.multiple_of(lax.rem(t, 2) * 8 * radii, 8 * radii), 8 * radii), :] = rows
            return carry

        lax.fori_loop(0, orders, one_order, 0)
        for step in far_first(n):
            back_copy(target(*step), me, c).start()
        got[c, me] = sums[c, me]
        return carry

    lax.fori_loop(0, chunks, chunk_step, 0)
    loads[3].wait()

    contract = (((1,), (1,)), ((), ()))
    own_group = me // halves
    for k in group_order(n, groups):
        g = lax.rem(own_group // k[2] + k[0], groups // k[2]) * k[2] + lax.rem(
            lax.rem(own_group, k[2]) + k[1], k[2]
        )
        rows = pl.ds(pl.multiple_of(g * radii, radii), radii)
        total = jnp.zeros((16 * radii, slots), jnp.float32)
        for h in range(halves):
            source = halves * g + h

            @pl.when(source != me)
            def _(source=source):
                for c in range(chunks):
                    back_copy(source, source, c).wait_recv()

            total += lax.dot_general(
                jnp.concatenate([got[c, source] for c in range(chunks)], axis=1),
                analysis[:, h * width : (h + 1) * width],
                contract, preferred_element_type=jnp.float32,
            )
        total = total.reshape(2, 4, 2, radii, slots)
        added = jnp.where(first, total[0], jnp.where(second, total[1], 0.0))
        last, start = [], []
        for f in range(4):
            scale = inner[2 * f : 2 * f + 1]
            for c in range(2):
                b = right[f, c, rows, :] + added[f, c]
                ahead, back = b, b
                ratio = rho[2 * f : 2 * f + 1]
                step = 1
                while step < radii:
                    ahead += ratio * jnp.where(at >= step, pltpu.roll(ahead, step, 0), 0.0)
                    back += ratio * jnp.where(
                        at < radii - step, pltpu.roll(back, radii - step, 0), 0.0
                    )
                    ratio = ratio * ratio
                    step *= 2
                right[f, c, rows, :] = scale * (ahead + back - b)
                last.append(ahead[radii - 1 : radii])
                start.append(back[0:1])
        carries[g, 0] = jnp.concatenate(last, axis=0)
        carries[g, 1] = jnp.concatenate(start, axis=0)

    hop = power(float(radii))
    ahead_at, back_at = [], []
    total = jnp.zeros((8, slots), jnp.float32)
    for g in range(groups):
        ahead_at.append(total)
        total = hop * total + carries[g, 0]
    edges[row, 0:8] = total
    total = jnp.zeros((8, slots), jnp.float32)
    for g in reversed(range(groups)):
        back_at.insert(0, total)
        total = hop * total + carries[g, 1]
    edges[row, 8:16] = total

    def edge_copy(e, source):
        return pltpu.make_async_remote_copy(
            src_ref=edges.at[row], dst_ref=edges.at[source],
            send_sem=edge_send.at[e], recv_sem=edge_recv.at[source],
            device_id={"row": e}, device_id_type=pl.DeviceIdType.MESH,
        )

    for k in range(1, rows_count):
        edge_copy(lax.rem(row + k, rows_count), row).start()

    before = (row * points).astype(jnp.float32)
    after = ((rows_count - 1 - row) * points).astype(jnp.float32)
    span = power(float(all_points + 1))
    scale = 1.0 / (1.0 - span * span)
    to_start, to_end = power(before), power(after)
    rise = [jnp.exp(log_rho[2 * f : 2 * f + 1] * near) for f in range(4)]
    fall = [jnp.exp(log_rho[2 * f : 2 * f + 1] * far) for f in range(4)]
    shifts = [power(float(k * points)) for k in range(rows_count)]
    inside = [power(float(k * radii)) for k in range(groups)]

    for c in range(chunks):
        for k in range(1, n):
            e = lax.rem(me + k, n)
            grid_copy(e, e, c).wait_send()
            back_copy(e, e, c).wait_send()
    for k in range(1, rows_count):
        e = lax.rem(row + k, rows_count)
        edge_copy(e, e).wait()

    zero = jnp.zeros((8, slots), jnp.float32)
    ahead_in, back_in, ahead_all, back_all = zero, zero, zero, zero
    for e in range(rows_count):
        f_e, g_e = edges[e, 0:8], edges[e, 8:16]
        weight, reverse = zero, zero
        for k in range(rows_count - 1):
            weight = jnp.where(row - 1 - e == k, shifts[k], weight)
            reverse = jnp.where(e - row - 1 == k, shifts[k], reverse)
        ahead_in += weight * f_e
        back_in += reverse * g_e
        ahead_all += shifts[rows_count - 1 - e] * f_e
        back_all += shifts[e] * g_e
    low = inner * rho * back_all
    high = inner * rho * ahead_all
    left = inner * ahead_in + (span * high - low) * scale * to_start
    rest = inner * back_in + (span * low - high) * scale * to_end
    for g in range(groups):
        here = left * inside[g] + inner * ahead_at[g]
        there = rest * inside[groups - 1 - g] + inner * back_at[g]
        for f in range(4):
            for c in range(2):
                i = 2 * f + c
                value = right[f, c, g * radii : (g + 1) * radii, :]
                value = value + here[i : i + 1] * rise[f] + there[i : i + 1] * fall[f]
                out[f, c, g * radii : (g + 1) * radii, :] = jnp.where(held, value, 0.0)


def group_order(n, groups):
    inner = 2 if groups % 2 == 0 and n == 2 * groups else 1
    steps = [(dy, dx, inner) for dy in range(groups // inner) for dx in range(inner)]
    return sorted(steps, key=lambda d: (d[0] > 0) + d[1])


def triad_table(pair_index):
    orders = jnp.stack([pair_index, LMAX - pair_index], axis=1).reshape(-1)
    count = orders.shape[0]
    need = orders[:, None] - orders[None, :]
    match = jnp.abs(need)[:, :, None] == orders[None, None, :]
    at = jnp.arange(count, dtype=jnp.int32)
    place = jnp.min(jnp.where(match, at, 3 * count), axis=2)
    place = jnp.where(jnp.logical_and(need < 0, place < count), place + count, place)
    place = jnp.where(need == orders[None, :], at[None, :] + 2 * count, place)
    return jnp.where(need > orders[None, :], 3 * count, place).reshape(-1)


def local(n, rows_count, spectra, dtheta, dphi, analysis, pair_index, diffusivity):
    points, slots = spectra.shape[2], spectra.shape[3]
    radii = RADII
    halves = n * radii // points
    width = -(-dtheta.shape[1] // (128 * halves)) * 128
    extra = width * halves - dtheta.shape[1]
    if extra:
        dtheta, dphi, analysis = (jnp.pad(v, ((0, 0), (0, extra))) for v in (dtheta, dphi, analysis))
    chunks = width // 128
    vmem = pl.BlockSpec(memory_space=pltpu.VMEM)
    smem = pl.BlockSpec(memory_space=pltpu.SMEM)
    hbm = pl.BlockSpec(memory_space=pltpu.HBM)
    shape = spectra.shape
    table = pltpu.VMEM(dtheta.shape, jnp.bfloat16)
    return pl.pallas_call(
        functools.partial(step_kernel, n, rows_count),
        out_shape=jax.ShapeDtypeStruct(shape, jnp.float32),
        in_specs=[smem, smem, smem, hbm, hbm, hbm, hbm],
        out_specs=vmem,
        scratch_shapes=[
            pltpu.VMEM(shape, jnp.float32),
            table,
            table,
            table,
            pltpu.VMEM((chunks, n, 24 * radii, 128), jnp.bfloat16),
            pltpu.VMEM((chunks, n, 24 * radii, 128), jnp.bfloat16),
            pltpu.VMEM((6 * n + 1, 12, radii, 128), jnp.float32),
            pltpu.VMEM((chunks, n, 16 * radii, 128), jnp.bfloat16),
            pltpu.VMEM((chunks, n, 16 * radii, 128), jnp.bfloat16),
            pltpu.VMEM((rows_count, 16, slots), jnp.float32),
            pltpu.VMEM(shape, jnp.float32),
            pltpu.VMEM((points // radii, 2, 8, slots), jnp.float32),
            pltpu.SemaphoreType.DMA((4,)),
            pltpu.SemaphoreType.DMA((chunks, n)),
            pltpu.SemaphoreType.DMA((chunks, n)),
            pltpu.SemaphoreType.DMA((chunks, n)),
            pltpu.SemaphoreType.DMA((chunks, n)),
            pltpu.SemaphoreType.DMA((rows_count,)),
            pltpu.SemaphoreType.DMA((rows_count,)),
        ],
        compiler_params=pltpu.CompilerParams(
            collective_id=0, has_side_effects=True, vmem_limit_bytes=VMEM_LIMIT
        ),
        name="step",
    )(triad_table(pair_index), pair_index, diffusivity, spectra, dtheta, dphi, analysis)


def solution(mesh):
    n, rows_count = mesh.shape["ma"], mesh.shape["row"]
    return jax.shard_map(
        functools.partial(local, n, rows_count),
        mesh=mesh,
        in_specs=(
            P(None, None, "row", "ma"),
            P("ma", None),
            P("ma", None),
            P("ma", None),
            P(),
            P(),
        ),
        out_specs=P(None, None, "row", "ma"),
        check_vma=False,
    )
```

profile of v0, /device:TPU:0, one launch (start us, length us, event | category | flops | bytes accessed | tf_op | source)
XLA Modules:
  0.0 43.8 jit_solution(6056947111430304905)
XLA Ops:
  0.0 0.0 copy-start
  0.0 0.7 %copy-done = s32[8]{0:T(128)S(1)} copy-done((s32[8]{0:T(128)S(1)}, s32[8]{0:T(128)}, u32[]{:S(2)}) %copy-start) | copy-done | bytes 56
  0.7 0.1 copy.9
  0.8 0.1 sub.30
  0.8 0.1 broadcast_in_dim.26
  0.9 0.1 subtract_abs_fusion
  1.0 0.4 select_reduce_fusion
  1.4 0.1 reduce_min.12
  1.5 0.1 sub.34
  1.6 0.1 sub.31
  1.7 0.1 sub.32
  1.8 0.6 %compare_select_fusion.1.partner = s32[256]{0:T(256)} fusion(s32[256]{0:T(256)S(1)} %sub.34, s32[256]{0:T(256)S(1)} %broadcast_in_dim.26, s32[256]{0:T(256)S(1)} %reduce_min.12, s32[256]{0:T(256)S(1)} %sub.32), kind=kLoop, calls=%fused_computation.4 | loop fusion | flops 2560 | bytes 5120 | tf_op jit(solution)/shard_map/jit(_where)/select_n | solution.py:389
  2.3 39.5 %step.1 = f32[4,2,32,528]{3,2,1,0:T(8,128)} custom-call(s32[256]{0:T(256)} %compare_select_fusion.1.partner, s32[8]{0:T(128)} %pair.1, f32[4]{0:T(128)} %diffusivity.1, f32[4,2,32,528]{3,2,1,0:T(8,128)} %spectra_hbm.1, bf16[528,768]{1,0:T(8,128)(2,1)} %dtheta_hbm.1, bf16[528,768]{1,0:T(8,128)(2,1)} %dphi_hbm.1, bf16[528,768]{1,0:T(8,128)(2,1)} %analysis_hbm.1), custom_call_target="tpu_custom_call" | custom-call | tf_op jit(solution)/shard_map/step/pallas_call | solution.py:406
  41.9 2.0 %copy.11 = f32[4,2,32,528]{3,2,1,0:T(8,128)} copy(f32[4,2,32,528]{3,2,1,0:T(8,128)} %step.1) | data formatting | bytes 1081344
  (5 shorter events, 0.0 us)
Async XLA Ops:
  0.0 0.7 %copy-start = (s32[8]{0:T(128)S(1)}, s32[8]{0:T(128)}, u32[]{:S(2)}) copy-start(s32[8]{0:T(128)} %pair.1) | copy-start | bytes 100
where the time goes:
time: 44 us; the launch traced here: 43.8 us
  Pallas kernels  39.5 us (90%)
  local copies, waits for them, and re-layouts  3.19 us (7%)
  other arithmetic  1.1 us (3%)
    pallas_call x1, Pallas kernels, local(): pl.pallas_call(functools.partial(step_kernel, n, rows_count), out_shape=j...  39.5 us
    unnamed x3, local copies, waits for them, and re-layouts  2.63 us

commit v1 on v0

v1 whole, which is shorter than its diff:
```python
import functools

import jax
import jax.numpy as jnp
from jax import lax
from jax.experimental import pallas as pl
from jax.experimental.pallas import tpu as pltpu
from jax.sharding import PartitionSpec as P

LMAX = 511
ROTATION = 2.0
SHELL_RADIUS = 16.0
RADII = 8
VMEM_LIMIT = 56 * 1024 * 1024
MESH = pl.DeviceIdType.MESH


def slot_rows(lowest, slots):
    slot = lax.broadcasted_iota(jnp.int32, (1, slots), 1)
    first = slot < LMAX + 1 - lowest
    held = slot < LMAX + 2
    second = jnp.logical_and(jnp.logical_not(first), held)
    degree = jnp.where(first, lowest + slot, slot - 1)
    order = jnp.where(first, lowest, LMAX - lowest)
    return first, second, held, degree, order


def say_hello(barrier, axis_sizes):
    total = 0
    for axis, size in axis_sizes:
        me = lax.axis_index(axis)
        for k in range(1, size):
            pl.semaphore_signal(
                barrier, inc=1, device_id={axis: lax.rem(me + k, size)}, device_id_type=MESH
            )
        total += size - 1
    return total


def partner_table(n, pair, out):
    count = 2 * n
    rows = lax.broadcasted_iota(jnp.int32, (count, 128), 0)
    lanes = lax.broadcasted_iota(jnp.int32, (count, 128), 1)
    values = []
    for g in range(n):
        values += [pair[g], LMAX - pair[g]]
    to = jnp.zeros((count, 128), jnp.int32)
    of = jnp.zeros((count, 128), jnp.int32)
    for k, value in enumerate(values):
        to = jnp.where(rows == k, value, to)
        of = jnp.where(lanes == k, value, of)
    need = to - of
    size = jnp.abs(need)
    place = jnp.full((count, 128), 3 * count, jnp.int32)
    for k, value in enumerate(values):
        place = jnp.where(size == value, k, place)
    place = jnp.where(jnp.logical_and(need < 0, place < count), place + count, place)
    place = jnp.where(need == of, lanes + 2 * count, place)
    out[...] = jnp.where(need > of, 3 * count, place)


def step_kernel(
    n, rows_count, pair, diffusivity, spectra_hbm, dtheta_hbm, dphi_hbm, analysis_hbm,
    local_out, ends_out,
    spectra, dtheta, dphi, analysis, send, x, states, sums, got, edges, right, ahead, back,
    partner_rows, partner,
    load_sem, table_sem, send_sem, recv_sem, back_send, back_recv, edge_send, edge_recv,
):
    loads = [
        pltpu.make_async_copy(source, target, load_sem.at[i])
        for i, (source, target) in enumerate(
            [(spectra_hbm, spectra), (dtheta_hbm, dtheta), (dphi_hbm, dphi), (analysis_hbm, analysis)]
        )
    ]
    for load in loads:
        load.start()
    barrier = pltpu.get_barrier_semaphore()
    greetings = say_hello(barrier, [("ma", n), ("row", rows_count)])
    me = lax.axis_index("ma")
    row = lax.axis_index("row")
    slots = spectra.shape[3]
    points = spectra.shape[2]
    radii = RADII
    groups = points // radii
    halves = n // groups
    width = dtheta.shape[1] // halves
    chunks = width // 128
    orders = 2 * n

    partner_table(n, pair, partner_rows)
    table_copy = pltpu.make_async_copy(partner_rows, partner, table_sem.at[0])
    table_copy.start()

    keep = jnp.where(pair[me] == 0, 0.0, 1.0).astype(jnp.float32)
    lowest = pair[me]
    first, second, held, degree, order = slot_rows(lowest, slots)

    for load in loads[:3]:
        load.wait()

    def block_for(group, half):
        v = spectra[:, :, group * radii : (group + 1) * radii, :]
        v = v.reshape(8 * radii, slots)
        lhs = jnp.concatenate([jnp.where(first, v, 0.0), jnp.where(second, v, 0.0)], axis=0)
        lhs = lhs.astype(jnp.bfloat16)
        columns = slice(half * width, (half + 1) * width)
        t = jnp.dot(lhs, dtheta[:, columns], preferred_element_type=jnp.float32)
        d = jnp.dot(lhs, dphi[:, columns], preferred_element_type=jnp.float32)
        t = t.reshape(2, 4, 2, radii, width)
        d = d.reshape(2, 4, 2, radii, width)
        parts = []
        for j in range(2):
            z_t, w_t, s_t, a_t = (t[j, f] for f in range(4))
            z_d, w_d, s_d, a_d = (d[j, f] for f in range(4))
            pieces = [
                (w_t[0] + z_d[1], w_t[1] - z_d[0]),
                (z_t[0] - w_d[1], z_t[1] + w_d[0]),
                (s_t[0], s_t[1]),
                (-s_d[1], s_d[0]),
                (a_d[1], -a_d[0]),
                (a_t[0], a_t[1]),
            ]
            for real, imag in pieces:
                parts += [real, imag * keep if j == 0 else imag]
        return jnp.concatenate(parts, axis=0).astype(jnp.bfloat16)

    for group in range(groups):
        for half in range(halves):
            value = block_for(group, half)
            for c in range(chunks):
                send[c, group * halves + half] = value[:, c * 128 : (c + 1) * 128]

    def grid_copy(e, source, c):
        return pltpu.make_async_remote_copy(
            src_ref=send.at[c, e], dst_ref=x.at[c, source],
            send_sem=send_sem.at[c, e], recv_sem=recv_sem.at[c, source],
            device_id={"ma": e}, device_id_type=MESH,
        )

    def back_copy(e, source, c):
        return pltpu.make_async_remote_copy(
            src_ref=sums.at[c, e], dst_ref=got.at[c, source],
            send_sem=back_send.at[c, e], recv_sem=back_recv.at[c, source],
            device_id={"ma": e}, device_id_type=MESH,
        )

    tall = n // 4
    my_y, my_x, my_core = me // 4, lax.rem(me // 2, 2), lax.rem(me, 2)

    def target(k):
        dy, dx, dc = k // 4, (k // 2) % 2, k % 2
        return (
            lax.rem(my_y + dy, tall) * 4 + lax.rem(my_x + dx, 2) * 2 + lax.rem(my_core + dc, 2)
        )

    pl.semaphore_wait(barrier, greetings)
    for c in range(chunks):
        for k in range(n - 1, 0, -1):
            grid_copy(target(k), me, c).start()
    for c in range(chunks):
        x[c, me] = send[c, me]

    alive = held.astype(jnp.float32)
    l = degree.astype(jnp.float32)
    m = order.astype(jnp.float32)
    lower = jnp.sqrt((l * l - m * m) * alive / jnp.maximum(4.0 * l * l - 1.0, 1.0)) * ROTATION
    u = l + 1.0
    upper = jnp.sqrt(jnp.maximum((u * u - m * m) / (4.0 * u * u - 1.0), 0.0))
    upper = jnp.where(degree < LMAX, upper * alive, 0.0) * ROTATION
    spin = ROTATION * m / (l * (l + 1.0) + 2.0) * alive

    all_points = points * rows_count
    field = lax.broadcasted_iota(jnp.int32, (8, 1), 0) // 2
    nu = jnp.zeros((8, 1), jnp.float32)
    for f in range(4):
        nu = jnp.where(field == f, diffusivity[f], nu)
    off = nu * float((all_points + 1) ** 2)
    half_excess = (1.0 + nu * (l * (l + 1.0) / SHELL_RADIUS**2)) / (2.0 * off)
    root = jnp.sqrt(half_excess * half_excess + 2.0 * half_excess)
    inverse = 1.0 + half_excess + root
    rho = 1.0 / inverse
    log_rho = -jnp.log(inverse)
    inner = 1.0 / (2.0 * off * root)

    def power(exponent):
        return jnp.exp(log_rho * exponent)

    def couple(v):
        edge = jnp.zeros((points, 1), jnp.float32)
        below = jnp.concatenate([edge, v[:, : slots - 1]], axis=1)
        above = jnp.concatenate([v[:, 1:], edge], axis=1)
        return (lower * below + upper * above) * alive

    z0, z1 = (jnp.where(held, spectra[0, c], 0.0) for c in range(2))
    w0, w1 = (jnp.where(held, spectra[1, c], 0.0) for c in range(2))
    linear = [
        z0 - spin * z1 + couple(w0),
        z1 + spin * z0 + couple(w1),
        w0 - spin * w1 - couple(z0),
        w1 + spin * w0 - couple(z1),
    ]
    for f in (2, 3):
        for c in range(2):
            linear.append(jnp.where(held, spectra[f, c], 0.0))
    for g in range(groups):
        block = jnp.stack([v[g * radii : (g + 1) * radii] for v in linear], axis=0)
        right[g * radii : (g + 1) * radii] = jnp.swapaxes(block, 0, 1)

    before = (row * points).astype(jnp.float32)
    after = ((rows_count - 1 - row) * points).astype(jnp.float32)

    zero = jnp.zeros((radii, 128), jnp.float32)
    for q in range(12):
        states[3 * orders, q] = zero
    table_copy.wait()

    def chunk_step(c, carry):
        def arrive(k, carry):
            e = lax.rem(me + k, n)
            grid_copy(e, e, c).wait_recv()
            return carry

        lax.fori_loop(1, n, arrive, 0)

        def unpack(g, carry):
            block = x[c, g].astype(jnp.float32).reshape(2, 6, 2, radii, 128)
            for j in range(2):
                at_order = 2 * g + j
                u_t, u_p, s_t, s_p, b_t, b_p = (block[j, q] for q in range(6))
                for q, (p, t) in enumerate(((b_p, b_t), (u_p, u_t), (s_p, s_t))):
                    plus = (p[0] - t[1], p[1] + t[0])
                    minus = (p[0] + t[1], p[1] - t[0])
                    parts = (plus[0], plus[1], minus[0], minus[1])
                    turned = (minus[0], -minus[1], plus[0], -plus[1])
                    for i in range(4):
                        states[at_order, 4 * q + i] = parts[i]
                        states[orders + at_order, 4 * q + i] = turned[i]
                        states[2 * orders + at_order, 4 * q + i] = 0.5 * parts[i]
            return carry

        lax.fori_loop(0, n, unpack, 0)

        def one_order(i, carry):
            e = target(n - 1 - i // 2)
            j = lax.rem(i, 2)
            t = 2 * e + j

            def add(a, total):
                b = partner[t, a]
                vp, vm, yp, ym, wp, wm = (
                    (states[a, 2 * q], states[a, 2 * q + 1], states[b, 2 * q], states[b, 2 * q + 1])
                    for q in range(6)
                )

                def square(v):
                    ar, ai, br, bi = v
                    return ar * br - ai * bi, ar * bi + ai * br

                def cross(v, w):
                    ar, ai, br, bi = v
                    cr, ci, dr, di = w
                    return (
                        (ar * dr - ai * di) + (cr * br - ci * bi),
                        (ar * di + ai * dr) + (cr * bi + ci * br),
                    )

                terms = []
                for v, y in ((vp, yp), (vm, ym)):
                    first_term, second_term = square(v), square(y)
                    terms += [first_term[0] - second_term[0], first_term[1] - second_term[1]]
                heat, other = cross(ym, wp), cross(yp, wm)
                terms += [heat[0] + other[0], heat[1] + other[1]]
                bent, other = cross(ym, vp), cross(yp, vm)
                terms += [bent[0] - other[0], bent[1] - other[1]]
                return tuple(v + w for v, w in zip(total, terms))

            pr, pi, mr, mi, hr, hi, er, ei = lax.fori_loop(0, orders, add, (zero,) * 8, unroll=8)
            rows = [pi - mi, mr - pr, pr + mr, pi + mi, -hr, -hi, ei, -er]
            block = jnp.swapaxes(jnp.stack(rows, axis=0), 0, 1).reshape(8 * radii, 128)
            block = (0.5 * block).astype(jnp.bfloat16)
            sums[c, e, pl.ds(pl.multiple_of(j * 8 * radii, 8 * radii), 8 * radii), :] = block

            @pl.when(jnp.logical_and(j == 1, i < orders - 2))
            def _():
                back_copy(e, me, c).start()

            return carry

        lax.fori_loop(0, orders, one_order, 0)
        got[c, me] = sums[c, me]
        return carry

    lax.fori_loop(0, chunks, chunk_step, 0)
    loads[3].wait()

    contract = (((1,), (1,)), ((), ()))

    def project(c):
        for k in range(1, n):
            e = lax.rem(me + k, n)
            back_copy(e, e, c).wait_recv()
        rhs = jnp.concatenate(
            [analysis[:, h * width + c * 128 : h * width + (c + 1) * 128] for h in range(halves)], axis=1
        )
        for g in range(groups):
            lhs = jnp.concatenate([got[c, g * halves + h] for h in range(halves)], axis=1)
            total = lax.dot_general(lhs, rhs, contract, preferred_element_type=jnp.float32)
            total = total.reshape(2, radii, 8, slots)
            rows = slice(g * radii, (g + 1) * radii)
            right[rows] += jnp.where(first, total[0], jnp.where(second, total[1], 0.0))

    for c in range(chunks):
        project(c)

    up = right[0]
    down = right[points - 1]
    ahead[0] = up
    back[points - 1] = down
    for k in range(1, points):
        up = right[k] + rho * up
        down = right[points - 1 - k] + rho * down
        ahead[k] = up
        back[points - 1 - k] = down
    edges[row] = jnp.concatenate([up, down], axis=0).astype(jnp.bfloat16)

    def edge_copy(e, source):
        return pltpu.make_async_remote_copy(
            src_ref=edges.at[row], dst_ref=edges.at[source],
            send_sem=edge_send.at[e], recv_sem=edge_recv.at[source],
            device_id={"row": e}, device_id_type=MESH,
        )

    for k in range(1, rows_count):
        edge_copy(lax.rem(row + k, rows_count), row).start()

    local_out[points - 1] = inner * ahead[points - 1]
    for k in range(points - 1):
        local_out[k] = inner * (ahead[k] + rho * back[k + 1])

    span = power(float(all_points + 1))
    scale = 1.0 / (1.0 - span * span)
    to_start, to_end = power(before), power(after)
    shifts = [power(float(k * points)) for k in range(rows_count)]
    zero = jnp.zeros((8, slots), jnp.float32)
    weights, reverses = [], []
    for e in range(rows_count):
        weight, reverse = zero, zero
        for k in range(rows_count - 1):
            weight = jnp.where(row - 1 - e == k, shifts[k], weight)
            reverse = jnp.where(e - row - 1 == k, shifts[k], reverse)
        weights.append(weight)
        reverses.append(reverse)
    ends_out[2] = rho

    for c in range(chunks):
        for k in range(1, n):
            e = lax.rem(me + k, n)
            grid_copy(e, e, c).wait_send()
            back_copy(e, e, c).wait_send()
    for k in range(1, rows_count):
        e = lax.rem(row + k, rows_count)
        edge_copy(e, e).wait()

    ahead_in, back_in, ahead_all, back_all = zero, zero, zero, zero
    for e in range(rows_count):
        both = edges[e].astype(jnp.float32)
        f_e, g_e = both[0:8], both[8:16]
        ahead_in += weights[e] * f_e
        back_in += reverses[e] * g_e
        ahead_all += shifts[rows_count - 1 - e] * f_e
        back_all += shifts[e] * g_e
    low = inner * rho * back_all
    high = inner * rho * ahead_all
    ends_out[0] = inner * ahead_in + (span * high - low) * scale * to_start
    ends_out[1] = inner * back_in + (span * low - high) * scale * to_end


def finish_kernel(inside, ends, out):
    points, slots = inside.shape[0], inside.shape[2]
    for start in range(0, slots, 128):
        at = slice(start, min(start + 128, slots))
        rho = ends[2, :, at]
        from_start, from_end = ends[0, :, at], ends[1, :, at]
        values = [inside[k, :, at] for k in range(points)]
        for k in range(points):
            from_start = from_start * rho
            values[k] = values[k] + from_start
        for k in reversed(range(points)):
            from_end = from_end * rho
            values[k] = values[k] + from_end
        for g in range(0, points, RADII):
            block = jnp.swapaxes(jnp.stack(values[g : g + RADII], axis=0), 0, 1)
            out[:, g : g + RADII, at] = block


def local(n, rows_count, spectra, dtheta, dphi, analysis, pair_index, diffusivity):
    points, slots = spectra.shape[2], spectra.shape[3]
    radii = RADII
    halves = n * radii // points
    width = -(-dtheta.shape[1] // (128 * halves)) * 128
    extra = width * halves - dtheta.shape[1]
    if extra:
        dtheta, dphi, analysis = (jnp.pad(v, ((0, 0), (0, extra))) for v in (dtheta, dphi, analysis))
    chunks = width // 128
    vmem = pl.BlockSpec(memory_space=pltpu.VMEM)
    smem = pl.BlockSpec(memory_space=pltpu.SMEM)
    hbm = pl.BlockSpec(memory_space=pltpu.HBM)
    shape = spectra.shape
    table = pltpu.VMEM(dtheta.shape, jnp.bfloat16)
    turned = pltpu.VMEM((points, 8, slots), jnp.float32)
    inside, ends = pl.pallas_call(
        functools.partial(step_kernel, n, rows_count),
        out_shape=(
            pltpu.VMEM((points, 8, slots), jnp.float32),
            pltpu.VMEM((3, 8, slots), jnp.float32),
        ),
        in_specs=[smem, smem, hbm, hbm, hbm, hbm],
        out_specs=(vmem, vmem),
        scratch_shapes=[
            pltpu.VMEM(shape, jnp.float32),
            table,
            table,
            table,
            pltpu.VMEM((chunks, n, 24 * radii, 128), jnp.bfloat16),
            pltpu.VMEM((chunks, n, 24 * radii, 128), jnp.bfloat16),
            pltpu.VMEM((6 * n + 1, 12, radii, 128), jnp.float32),
            pltpu.VMEM((chunks, n, 16 * radii, 128), jnp.bfloat16),
            pltpu.VMEM((chunks, n, 16 * radii, 128), jnp.bfloat16),
            pltpu.VMEM((rows_count, 16, slots), jnp.bfloat16),
            turned,
            turned,
            turned,
            pltpu.VMEM((2 * n, 128), jnp.int32),
            pltpu.SMEM((2 * n, 128), jnp.int32),
            pltpu.SemaphoreType.DMA((4,)),
            pltpu.SemaphoreType.DMA((1,)),
            pltpu.SemaphoreType.DMA((chunks, n)),
            pltpu.SemaphoreType.DMA((chunks, n)),
            pltpu.SemaphoreType.DMA((chunks, n)),
            pltpu.SemaphoreType.DMA((chunks, n)),
            pltpu.SemaphoreType.DMA((rows_count,)),
            pltpu.SemaphoreType.DMA((rows_count,)),
        ],
        compiler_params=pltpu.CompilerParams(
            collective_id=0, has_side_effects=True, vmem_limit_bytes=VMEM_LIMIT
        ),
        name="step",
    )(pair_index, diffusivity, spectra, dtheta, dphi, analysis)
    result = pl.pallas_call(
        finish_kernel,
        out_shape=jax.ShapeDtypeStruct((8, points, slots), jnp.float32),
        in_specs=[vmem, vmem],
        out_specs=vmem,
        compiler_params=pltpu.CompilerParams(vmem_limit_bytes=8 * 1024 * 1024),
        name="finish",
    )(inside, ends)
    return result.reshape(shape)


def solution(mesh):
    n, rows_count = mesh.shape["ma"], mesh.shape["row"]
    return jax.shard_map(
        functools.partial(local, n, rows_count),
        mesh=mesh,
        in_specs=(
            P(None, None, "row", "ma"),
            P("ma", None),
            P("ma", None),
            P("ma", None),
            P(),
            P(),
        ),
        out_specs=P(None, None, "row", "ma"),
        check_vma=False,
    )
```

time: 44 us -> 37.2 us (0.85)
  local copies, waits for them, and re-layouts: 3.19 us -> 0 us
  Pallas kernels: 39.5 us -> 37.1 us
  other arithmetic: 1.1 us -> 0 us
    unnamed x3 -> x0, local copies, waits for them, and re-layouts: 2.63 us -> none
    pallas_call x1 -> x2, Pallas kernels: 39.5 us -> 37.1 us  [the longest x1 36 us: local(): pl.pallas_call(functools.partial(step_kernel, n, rows_count), out_shape=(...]
    select_n x1 -> x0, other arithmetic: 0.58 us -> none  [triad_table(): return jnp.where(need > orders[None, :], 3 * count, place).reshape(-1)]
where the time goes in v1:
time: 37.2 us; the launch traced here: 37.1 us
  Pallas kernels  37.1 us (100%)
    pallas_call x1, Pallas kernels, local(): pl.pallas_call(functools.partial(step_kernel, n, rows_count), out_shape=(...  36 us
    pallas_call x1, Pallas kernels, local(): pl.pallas_call(finish_kernel, out_shape=jax.ShapeDtypeStruct((8, points,...  1.05 us

profile of v1, /device:TPU:0, one launch (start us, length us, event | category | flops | bytes accessed | tf_op | source)
XLA Modules:
  0.0 37.1 jit_solution(8011922451197370102)
XLA Ops:
  0.0 36.0 %step.1 = (f32[32,8,528]{2,1,0:T(8,128)S(1)}, f32[3,8,528]{2,1,0:T(8,128)S(1)}) custom-call(s32[8]{0:T(128)} %pair.1, f32[4]{0:T(128)} %diffusivity.1, f32[4,2,32,528]{3,2,1,0:T(8,128)} %spectra_hbm.1, bf16[528,768]{1,0:T(8,128)(2,1)} %dtheta_hbm.1, bf16[528,768]{1,0:T(8,128)(2,1)} %dphi_hbm.1, bf16[528,768]{1,0:T(8,128)(2,1)} %analysis_hbm.1), custom_call_target="tpu_custom_call" | custom-call | tf_op jit(solution)/shard_map/step/pallas_call | solution.py:411
  36.0 1.1 %finish.1 = f32[8,32,528]{2,1,0:T(8,128)} custom-call(f32[32,8,528]{2,1,0:T(8,128)S(1)} %get-tuple-element.7.inside, f32[3,8,528]{2,1,0:T(8,128)S(1)} %get-tuple-element.8.ends), custom_call_target="tpu_custom_call" | custom-call | tf_op jit(solution)/shard_map/finish/pallas_call | solution.py:449

commit v2 on v1

--- a/solution.py
+++ b/solution.py
@@ -60,22 +60,25 @@
 
 
 def step_kernel(
-    n, rows_count, pair, diffusivity, spectra_hbm, dtheta_hbm, dphi_hbm, analysis_hbm,
-    local_out, ends_out,
+    n, rows_count, pair_hbm, diffusivity_hbm, spectra_hbm, dtheta_hbm, dphi_hbm, analysis_hbm,
+    local_out, ends_out, rise, fall,
     spectra, dtheta, dphi, analysis, send, x, states, sums, got, edges, right, ahead, back,
-    partner_rows, partner,
+    partner_rows, partner, pair, diffusivity,
     load_sem, table_sem, send_sem, recv_sem, back_send, back_recv, edge_send, edge_recv,
 ):
     loads = [
         pltpu.make_async_copy(source, target, load_sem.at[i])
         for i, (source, target) in enumerate(
-            [(spectra_hbm, spectra), (dtheta_hbm, dtheta), (dphi_hbm, dphi), (analysis_hbm, analysis)]
+            [
+                (pair_hbm, pair), (spectra_hbm, spectra), (dtheta_hbm, dtheta), (dphi_hbm, dphi),
+                (diffusivity_hbm, diffusivity), (analysis_hbm, analysis),
+            ]
         )
     ]
+    barrier = pltpu.get_barrier_semaphore()
+    greetings = say_hello(barrier, [("ma", n), ("row", rows_count)])
     for load in loads:
         load.start()
-    barrier = pltpu.get_barrier_semaphore()
-    greetings = say_hello(barrier, [("ma", n), ("row", rows_count)])
     me = lax.axis_index("ma")
     row = lax.axis_index("row")
     slots = spectra.shape[3]
@@ -87,6 +90,7 @@
     chunks = width // 128
     orders = 2 * n
 
+    loads[0].wait()
     partner_table(n, pair, partner_rows)
     table_copy = pltpu.make_async_copy(partner_rows, partner, table_sem.at[0])
     table_copy.start()
@@ -95,19 +99,14 @@
     lowest = pair[me]
     first, second, held, degree, order = slot_rows(lowest, slots)
 
-    for load in loads[:3]:
-        load.wait()
-
-    def block_for(group, half):
-        v = spectra[:, :, group * radii : (group + 1) * radii, :]
-        v = v.reshape(8 * radii, slots)
-        lhs = jnp.concatenate([jnp.where(first, v, 0.0), jnp.where(second, v, 0.0)], axis=0)
-        lhs = lhs.astype(jnp.bfloat16)
-        columns = slice(half * width, (half + 1) * width)
-        t = jnp.dot(lhs, dtheta[:, columns], preferred_element_type=jnp.float32)
-        d = jnp.dot(lhs, dphi[:, columns], preferred_element_type=jnp.float32)
-        t = t.reshape(2, 4, 2, radii, width)
-        d = d.reshape(2, 4, 2, radii, width)
+    loads[1].wait()
+    lhs = []
+    for g in range(groups):
+        v = spectra[:, :, g * radii : (g + 1) * radii, :].reshape(8 * radii, slots)
+        lhs += [jnp.where(first, v, 0.0), jnp.where(second, v, 0.0)]
+    lhs = jnp.concatenate(lhs, axis=0).astype(jnp.bfloat16)
+
+    def grid_block(t, d):
         parts = []
         for j in range(2):
             z_t, w_t, s_t, a_t = (t[j, f] for f in range(4))
@@ -124,11 +123,21 @@
                 parts += [real, imag * keep if j == 0 else imag]
         return jnp.concatenate(parts, axis=0).astype(jnp.bfloat16)
 
-    for group in range(groups):
-        for half in range(halves):
-            value = block_for(group, half)
-            for c in range(chunks):
-                send[c, group * halves + half] = value[:, c * 128 : (c + 1) * 128]
+    loads[2].wait()
+    loads[3].wait()
+    block = 256 if (width * halves) % 256 == 0 else 128
+    for start in range(0, width * halves, block):
+        t, d = (
+            jnp.dot(lhs, v[:, start : start + block], preferred_element_type=jnp.float32)
+            for v in (dtheta, dphi)
+        )
+        t = t.reshape(groups, 2, 4, 2, radii, block)
+        d = d.reshape(groups, 2, 4, 2, radii, block)
+        for at in range(start, start + block, 128):
+            half, c = at // width, at % width // 128
+            here = slice(at - start, at - start + 128)
+            for g in range(groups):
+                send[c, g * halves + half] = grid_block(t[g, ..., here], d[g, ..., here])
 
     def grid_copy(e, source, c):
         return pltpu.make_async_remote_copy(
@@ -169,6 +178,7 @@
     upper = jnp.where(degree < LMAX, upper * alive, 0.0) * ROTATION
     spin = ROTATION * m / (l * (l + 1.0) + 2.0) * alive
 
+    loads[4].wait()
     all_points = points * rows_count
     field = lax.broadcasted_iota(jnp.int32, (8, 1), 0) // 2
     nu = jnp.zeros((8, 1), jnp.float32)
@@ -206,6 +216,12 @@
         block = jnp.stack([v[g * radii : (g + 1) * radii] for v in linear], axis=0)
         right[g * radii : (g + 1) * radii] = jnp.swapaxes(block, 0, 1)
 
+    at = lax.broadcasted_iota(jnp.int32, (points, slots), 0)
+    for f in range(4):
+        log_here = log_rho[2 * f : 2 * f + 1]
+        rise[f] = jnp.exp(log_here * (at + 1).astype(jnp.float32))
+        fall[f] = jnp.exp(log_here * (points - at).astype(jnp.float32))
+
     before = (row * points).astype(jnp.float32)
     after = ((rows_count - 1 - row) * points).astype(jnp.float32)
 
@@ -215,14 +231,13 @@
     table_copy.wait()
 
     def chunk_step(c, carry):
-        def arrive(k, carry):
-            e = lax.rem(me + k, n)
-            grid_copy(e, e, c).wait_recv()
-            return carry
-
-        lax.fori_loop(1, n, arrive, 0)
-
-        def unpack(g, carry):
+        def unpack(k, carry):
+            g = target(k)
+
+            @pl.when(k > 0)
+            def _():
+                grid_copy(g, g, c).wait_recv()
+
             block = x[c, g].astype(jnp.float32).reshape(2, 6, 2, radii, 128)
             for j in range(2):
                 at_order = 2 * g + j
@@ -291,7 +306,7 @@
         return carry
 
     lax.fori_loop(0, chunks, chunk_step, 0)
-    loads[3].wait()
+    loads[5].wait()
 
     contract = (((1,), (1,)), ((), ()))
 
@@ -333,9 +348,12 @@
     for k in range(1, rows_count):
         edge_copy(lax.rem(row + k, rows_count), row).start()
 
-    local_out[points - 1] = inner * ahead[points - 1]
-    for k in range(points - 1):
-        local_out[k] = inner * (ahead[k] + rho * back[k + 1])
+    for g in range(groups):
+        values = []
+        for k in range(g * radii, (g + 1) * radii):
+            value = ahead[k] + rho * back[k + 1] if k < points - 1 else ahead[k]
+            values.append(inner * value)
+        local_out[:, g * radii : (g + 1) * radii] = jnp.swapaxes(jnp.stack(values, axis=0), 0, 1)
 
     span = power(float(all_points + 1))
     scale = 1.0 / (1.0 - span * span)
@@ -350,7 +368,6 @@
             reverse = jnp.where(e - row - 1 == k, shifts[k], reverse)
         weights.append(weight)
         reverses.append(reverse)
-    ends_out[2] = rho
 
     for c in range(chunks):
         for k in range(1, n):
@@ -375,22 +392,15 @@
     ends_out[1] = inner * back_in + (span * low - high) * scale * to_end
 
 
-def finish_kernel(inside, ends, out):
-    points, slots = inside.shape[0], inside.shape[2]
-    for start in range(0, slots, 128):
-        at = slice(start, min(start + 128, slots))
-        rho = ends[2, :, at]
-        from_start, from_end = ends[0, :, at], ends[1, :, at]
-        values = [inside[k, :, at] for k in range(points)]
-        for k in range(points):
-            from_start = from_start * rho
-            values[k] = values[k] + from_start
-        for k in reversed(range(points)):
-            from_end = from_end * rho
-            values[k] = values[k] + from_end
-        for g in range(0, points, RADII):
-            block = jnp.swapaxes(jnp.stack(values[g : g + RADII], axis=0), 0, 1)
-            out[:, g : g + RADII, at] = block
+def finish_kernel(inside, ends, rise, fall, out, result, sem):
+    copies = []
+    for q in range(8):
+        left, right = ends[0, q : q + 1], ends[1, q : q + 1]
+        result[q] = inside[q] + left * rise[q // 2] + right * fall[q // 2]
+        copies.append(pltpu.make_async_copy(result.at[q], out.at[q], sem.at[q]))
+        copies[-1].start()
+    for copy in copies:
+        copy.wait()
 
 
 def local(n, rows_count, spectra, dtheta, dphi, analysis, pair_index, diffusivity):
@@ -403,19 +413,20 @@
         dtheta, dphi, analysis = (jnp.pad(v, ((0, 0), (0, extra))) for v in (dtheta, dphi, analysis))
     chunks = width // 128
     vmem = pl.BlockSpec(memory_space=pltpu.VMEM)
-    smem = pl.BlockSpec(memory_space=pltpu.SMEM)
     hbm = pl.BlockSpec(memory_space=pltpu.HBM)
     shape = spectra.shape
     table = pltpu.VMEM(dtheta.shape, jnp.bfloat16)
     turned = pltpu.VMEM((points, 8, slots), jnp.float32)
-    inside, ends = pl.pallas_call(
+    inside, ends, rise, fall = pl.pallas_call(
         functools.partial(step_kernel, n, rows_count),
         out_shape=(
-            pltpu.VMEM((points, 8, slots), jnp.float32),
-            pltpu.VMEM((3, 8, slots), jnp.float32),
+            pltpu.VMEM((8, points, slots), jnp.float32),
+            pltpu.VMEM((2, 8, slots), jnp.float32),
+            pltpu.VMEM((4, points, slots), jnp.float32),
+            pltpu.VMEM((4, points, slots), jnp.float32),
         ),
-        in_specs=[smem, smem, hbm, hbm, hbm, hbm],
-        out_specs=(vmem, vmem),
+        in_specs=[hbm] * 6,
+        out_specs=(vmem,) * 4,
         scratch_shapes=[
             pltpu.VMEM(shape, jnp.float32),
             table,
@@ -432,7 +443,9 @@
             turned,
             pltpu.VMEM((2 * n, 128), jnp.int32),
             pltpu.SMEM((2 * n, 128), jnp.int32),
-            pltpu.SemaphoreType.DMA((4,)),
+            pltpu.SMEM(pair_index.shape, jnp.int32),
+            pltpu.SMEM(diffusivity.shape, jnp.float32),
+            pltpu.SemaphoreType.DMA((6,)),
             pltpu.SemaphoreType.DMA((1,)),
             pltpu.SemaphoreType.DMA((chunks, n)),
             pltpu.SemaphoreType.DMA((chunks, n)),
@@ -449,11 +462,14 @@
     result = pl.pallas_call(
         finish_kernel,
         out_shape=jax.ShapeDtypeStruct((8, points, slots), jnp.float32),
-        in_specs=[vmem, vmem],
-        out_specs=vmem,
+        in_specs=[vmem] * 4,
+        out_specs=hbm,
+        scratch_shapes=[
+            pltpu.VMEM((8, points, slots), jnp.float32), pltpu.SemaphoreType.DMA((8,))
+        ],
         compiler_params=pltpu.CompilerParams(vmem_limit_bytes=8 * 1024 * 1024),
         name="finish",
-    )(inside, ends)
+    )(inside, ends, rise, fall)
     return result.reshape(shape)
 
 

time: 37.2 us -> 36.1 us (0.970)
  Pallas kernels: 37.1 us -> 35.9 us
    pallas_call x1, Pallas kernels: 36 us -> 35 us  [local(): pl.pallas_call(functools.partial(step_kernel, n, rows_count), out_shape=(...]
where the time goes in v2:
time: 36.1 us; the launch traced here: 35.9 us
  Pallas kernels  35.9 us (99%)
    pallas_call x1, Pallas kernels, local(): pl.pallas_call(functools.partial(step_kernel, n, rows_count), out_shape=(...  35 us
    pallas_call x1, Pallas kernels, local(): pl.pallas_call(finish_kernel, out_shape=jax.ShapeDtypeStruct((8, points,...  0.92 us

profile of v2, /device:TPU:0, one launch (start us, length us, event | category | flops | bytes accessed | tf_op | source)
XLA Modules:
  0.0 35.9 jit_solution(9727664664205261465)
XLA Ops:
  0.0 35.0 %step.1 = (f32[8,32,528]{2,1,0:T(8,128)S(1)}, f32[2,8,528]{2,1,0:T(8,128)S(1)}, f32[4,32,528]{2,1,0:T(8,128)S(1)}, f32[4,32,528]{2,1,0:T(8,128)S(1)}) custom-call(s32[8]{0:T(128)} %pair_hbm.1, f32[4]{0:T(128)} %diffusivity_hbm.1, f32[4,2,32,528]{3,2,1,0:T(8,128)} %spectra_hbm.1, bf16[528,768]{1,0:T(8,128)(2,1)} %dtheta_hbm.1, bf16[528,768]{1,0:T(8,128)(2,1)} %dphi_hbm.1, ...), custom_call_target="tpu_custom_call" | custom-call | tf_op jit(solution)/shard_map/step/pallas_call | solution.py:420
  35.0 0.9 %finish.1 = f32[8,32,528]{2,1,0:T(8,128)} custom-call(f32[8,32,528]{2,1,0:T(8,128)S(1)} %get-tuple-element.9.inside, f32[2,8,528]{2,1,0:T(8,128)S(1)} %get-tuple-element.10.ends, f32[4,32,528]{2,1,0:T(8,128)S(1)} %get-tuple-element.11.rise, f32[4,32,528]{2,1,0:T(8,128)S(1)} %get-tuple-element.12.fall), custom_call_target="tpu_custom_call" | custom-call | tf_op jit(solution)/shard_map/finish/pallas_call | solution.py:462

commit v3 on v2

--- a/solution.py
+++ b/solution.py
@@ -64,21 +64,8 @@
     local_out, ends_out, rise, fall,
     spectra, dtheta, dphi, analysis, send, x, states, sums, got, edges, right, ahead, back,
     partner_rows, partner, pair, diffusivity,
-    load_sem, table_sem, send_sem, recv_sem, back_send, back_recv, edge_send, edge_recv,
+    load_sem, piece_sem, table_sem, send_sem, recv_sem, back_send, back_recv, edge_send, edge_recv,
 ):
-    loads = [
-        pltpu.make_async_copy(source, target, load_sem.at[i])
-        for i, (source, target) in enumerate(
-            [
-                (pair_hbm, pair), (spectra_hbm, spectra), (dtheta_hbm, dtheta), (dphi_hbm, dphi),
-                (diffusivity_hbm, diffusivity), (analysis_hbm, analysis),
-            ]
-        )
-    ]
-    barrier = pltpu.get_barrier_semaphore()
-    greetings = say_hello(barrier, [("ma", n), ("row", rows_count)])
-    for load in loads:
-        load.start()
     me = lax.axis_index("ma")
     row = lax.axis_index("row")
     slots = spectra.shape[3]
@@ -86,9 +73,35 @@
     radii = RADII
     groups = points // radii
     halves = n // groups
-    width = dtheta.shape[1] // halves
-    chunks = width // 128
+    chunks = dtheta.shape[0]
+    width = chunks * 128
     orders = 2 * n
+
+    def piece(i, c, h):
+        source, place = ((dtheta_hbm, dtheta), (dphi_hbm, dphi), (analysis_hbm, analysis))[i]
+        columns = slice(h * width + c * 128, h * width + (c + 1) * 128)
+        return pltpu.make_async_copy(
+            source.at[:, columns], place.at[c, :, h * 128 : (h + 1) * 128], piece_sem.at[i, c, h]
+        )
+
+    loads = [
+        pltpu.make_async_copy(source, place, load_sem.at[i])
+        for i, (source, place) in enumerate(
+            [(pair_hbm, pair), (spectra_hbm, spectra), (diffusivity_hbm, diffusivity)]
+        )
+    ]
+    barrier = pltpu.get_barrier_semaphore()
+    greetings = say_hello(barrier, [("ma", n), ("row", rows_count)])
+    loads[0].start()
+    loads[1].start()
+    for c in range(chunks):
+        for h in range(halves):
+            piece(0, c, h).start()
+            piece(1, c, h).start()
+    loads[2].start()
+    for c in range(chunks):
+        for h in range(halves):
+            piece(2, c, h).start()
 
     loads[0].wait()
     partner_table(n, pair, partner_rows)
@@ -123,22 +136,6 @@
                 parts += [real, imag * keep if j == 0 else imag]
         return jnp.concatenate(parts, axis=0).astype(jnp.bfloat16)
 
-    loads[2].wait()
-    loads[3].wait()
-    block = 256 if (width * halves) % 256 == 0 else 128
-    for start in range(0, width * halves, block):
-        t, d = (
-            jnp.dot(lhs, v[:, start : start + block], preferred_element_type=jnp.float32)
-            for v in (dtheta, dphi)
-        )
-        t = t.reshape(groups, 2, 4, 2, radii, block)
-        d = d.reshape(groups, 2, 4, 2, radii, block)
-        for at in range(start, start + block, 128):
-            half, c = at // width, at % width // 128
-            here = slice(at - start, at - start + 128)
-            for g in range(groups):
-                send[c, g * halves + half] = grid_block(t[g, ..., here], d[g, ..., here])
-
     def grid_copy(e, source, c):
         return pltpu.make_async_remote_copy(
             src_ref=send.at[c, e], dst_ref=x.at[c, source],
@@ -162,12 +159,30 @@
             lax.rem(my_y + dy, tall) * 4 + lax.rem(my_x + dx, 2) * 2 + lax.rem(my_core + dc, 2)
         )
 
-    pl.semaphore_wait(barrier, greetings)
     for c in range(chunks):
+        for h in range(halves):
+            piece(0, c, h).wait()
+            piece(1, c, h).wait()
+        t, d = (jnp.dot(lhs, v[c], preferred_element_type=jnp.float32) for v in (dtheta, dphi))
+        t = t.reshape(groups, 2, 4, 2, radii, halves * 128)
+        d = d.reshape(groups, 2, 4, 2, radii, halves * 128)
+        for g in range(groups):
+            for h in range(halves):
+                here = slice(h * 128, (h + 1) * 128)
+                send[c, g * halves + h] = grid_block(t[g, ..., here], d[g, ..., here])
+        if c == 0:
+            pl.semaphore_wait(barrier, greetings)
         for k in range(n - 1, 0, -1):
             grid_copy(target(k), me, c).start()
-    for c in range(chunks):
         x[c, me] = send[c, me]
+
+    near_first = sorted(range(n), key=lambda e: (e // 4 + e // 2 % 2 + e % 2, -e))
+
+    def served(k):
+        e = near_first[0]
+        for at in range(1, n):
+            e = jnp.where(k == at, near_first[at], e)
+        return e
 
     alive = held.astype(jnp.float32)
     l = degree.astype(jnp.float32)
@@ -178,7 +193,7 @@
     upper = jnp.where(degree < LMAX, upper * alive, 0.0) * ROTATION
     spin = ROTATION * m / (l * (l + 1.0) + 2.0) * alive
 
-    loads[4].wait()
+    loads[2].wait()
     all_points = points * rows_count
     field = lax.broadcasted_iota(jnp.int32, (8, 1), 0) // 2
     nu = jnp.zeros((8, 1), jnp.float32)
@@ -256,7 +271,7 @@
         lax.fori_loop(0, n, unpack, 0)
 
         def one_order(i, carry):
-            e = target(n - 1 - i // 2)
+            e = served(i // 2)
             j = lax.rem(i, 2)
             t = 2 * e + j
 
@@ -295,7 +310,7 @@
             block = (0.5 * block).astype(jnp.bfloat16)
             sums[c, e, pl.ds(pl.multiple_of(j * 8 * radii, 8 * radii), 8 * radii), :] = block
 
-            @pl.when(jnp.logical_and(j == 1, i < orders - 2))
+            @pl.when(jnp.logical_and(j == 1, e != me))
             def _():
                 back_copy(e, me, c).start()
 
@@ -306,7 +321,9 @@
         return carry
 
     lax.fori_loop(0, chunks, chunk_step, 0)
-    loads[5].wait()
+    for c in range(chunks):
+        for h in range(halves):
+            piece(2, c, h).wait()
 
     contract = (((1,), (1,)), ((), ()))
 
@@ -314,12 +331,9 @@
         for k in range(1, n):
             e = lax.rem(me + k, n)
             back_copy(e, e, c).wait_recv()
-        rhs = jnp.concatenate(
-            [analysis[:, h * width + c * 128 : h * width + (c + 1) * 128] for h in range(halves)], axis=1
-        )
         for g in range(groups):
             lhs = jnp.concatenate([got[c, g * halves + h] for h in range(halves)], axis=1)
-            total = lax.dot_general(lhs, rhs, contract, preferred_element_type=jnp.float32)
+            total = lax.dot_general(lhs, analysis[c], contract, preferred_element_type=jnp.float32)
             total = total.reshape(2, radii, 8, slots)
             rows = slice(g * radii, (g + 1) * radii)
             right[rows] += jnp.where(first, total[0], jnp.where(second, total[1], 0.0))
@@ -415,7 +429,7 @@
     vmem = pl.BlockSpec(memory_space=pltpu.VMEM)
     hbm = pl.BlockSpec(memory_space=pltpu.HBM)
     shape = spectra.shape
-    table = pltpu.VMEM(dtheta.shape, jnp.bfloat16)
+    table = pltpu.VMEM((chunks, slots, halves * 128), jnp.bfloat16)
     turned = pltpu.VMEM((points, 8, slots), jnp.float32)
     inside, ends, rise, fall = pl.pallas_call(
         functools.partial(step_kernel, n, rows_count),
@@ -445,7 +459,8 @@
             pltpu.SMEM((2 * n, 128), jnp.int32),
             pltpu.SMEM(pair_index.shape, jnp.int32),
             pltpu.SMEM(diffusivity.shape, jnp.float32),
-            pltpu.SemaphoreType.DMA((6,)),
+            pltpu.SemaphoreType.DMA((3,)),
+            pltpu.SemaphoreType.DMA((3, chunks, halves)),
             pltpu.SemaphoreType.DMA((1,)),
             pltpu.SemaphoreType.DMA((chunks, n)),
             pltpu.SemaphoreType.DMA((chunks, n)),

time: 36.1 us -> 35.3 us (0.978)
  Pallas kernels: 35.9 us -> 35.2 us
    pallas_call x1, Pallas kernels: 35 us -> 34.3 us  [local(): pl.pallas_call(functools.partial(step_kernel, n, rows_count), out_shape=(...]
where the time goes in v3:
time: 35.3 us; the launch traced here: 35.2 us
  Pallas kernels  35.2 us (100%)
    pallas_call x1, Pallas kernels, local(): pl.pallas_call(functools.partial(step_kernel, n, rows_count), out_shape=(...  34.3 us
    pallas_call x1, Pallas kernels, local(): pl.pallas_call(finish_kernel, out_shape=jax.ShapeDtypeStruct((8, points,...  0.92 us

profile of v3, /device:TPU:0, one launch (start us, length us, event | category | flops | bytes accessed | tf_op | source)
XLA Modules:
  0.0 35.2 jit_solution(5430324419887171192)
XLA Ops:
  0.0 34.3 %step.1 = (f32[8,32,528]{2,1,0:T(8,128)S(1)}, f32[2,8,528]{2,1,0:T(8,128)S(1)}, f32[4,32,528]{2,1,0:T(8,128)S(1)}, f32[4,32,528]{2,1,0:T(8,128)S(1)}) custom-call(s32[8]{0:T(128)} %pair_hbm.1, f32[4]{0:T(128)} %diffusivity_hbm.1, f32[4,2,32,528]{3,2,1,0:T(8,128)} %spectra_hbm.1, bf16[528,768]{1,0:T(8,128)(2,1)} %dtheta_hbm.1, bf16[528,768]{1,0:T(8,128)(2,1)} %dphi_hbm.1, ...), custom_call_target="tpu_custom_call" | custom-call | tf_op jit(solution)/shard_map/step/pallas_call | solution.py:434
  34.3 0.9 %finish.1 = f32[8,32,528]{2,1,0:T(8,128)} custom-call(f32[8,32,528]{2,1,0:T(8,128)S(1)} %get-tuple-element.9.inside, f32[2,8,528]{2,1,0:T(8,128)S(1)} %get-tuple-element.10.ends, f32[4,32,528]{2,1,0:T(8,128)S(1)} %get-tuple-element.11.rise, f32[4,32,528]{2,1,0:T(8,128)S(1)} %get-tuple-element.12.fall), custom_call_target="tpu_custom_call" | custom-call | tf_op jit(solution)/shard_map/finish/pallas_call | solution.py:477

commit v4 on v3

--- a/solution.py
+++ b/solution.py
@@ -62,7 +62,7 @@
 def step_kernel(
     n, rows_count, pair_hbm, diffusivity_hbm, spectra_hbm, dtheta_hbm, dphi_hbm, analysis_hbm,
     local_out, ends_out, rise, fall,
-    spectra, dtheta, dphi, analysis, send, x, states, sums, got, edges, right, ahead, back,
+    spectra, dtheta, dphi, analysis, turned_table, send, x, states, sums, got, edges, right, ahead, back,
     partner_rows, partner, pair, diffusivity,
     load_sem, piece_sem, table_sem, send_sem, recv_sem, back_send, back_recv, edge_send, edge_recv,
 ):
@@ -94,19 +94,21 @@
     greetings = say_hello(barrier, [("ma", n), ("row", rows_count)])
     loads[0].start()
     loads[1].start()
-    for c in range(chunks):
-        for h in range(halves):
-            piece(0, c, h).start()
-            piece(1, c, h).start()
-    loads[2].start()
-    for c in range(chunks):
-        for h in range(halves):
-            piece(2, c, h).start()
+    for h in range(halves):
+        piece(0, 0, h).start()
+        piece(1, 0, h).start()
+
+    def load_rest():
+        for i in range(2):
+            for c in range(1, chunks):
+                for h in range(halves):
+                    piece(i, c, h).start()
+        loads[2].start()
+        for c in range(chunks):
+            for h in range(halves):
+                piece(2, c, h).start()
 
     loads[0].wait()
-    partner_table(n, pair, partner_rows)
-    table_copy = pltpu.make_async_copy(partner_rows, partner, table_sem.at[0])
-    table_copy.start()
 
     keep = jnp.where(pair[me] == 0, 0.0, 1.0).astype(jnp.float32)
     lowest = pair[me]
@@ -116,8 +118,8 @@
     lhs = []
     for g in range(groups):
         v = spectra[:, :, g * radii : (g + 1) * radii, :].reshape(8 * radii, slots)
-        lhs += [jnp.where(first, v, 0.0), jnp.where(second, v, 0.0)]
-    lhs = jnp.concatenate(lhs, axis=0).astype(jnp.bfloat16)
+        v = jnp.concatenate([jnp.where(first, v, 0.0), jnp.where(second, v, 0.0)], axis=0)
+        lhs.append(v.astype(jnp.bfloat16))
 
     def grid_block(t, d):
         parts = []
@@ -163,18 +165,44 @@
         for h in range(halves):
             piece(0, c, h).wait()
             piece(1, c, h).wait()
-        t, d = (jnp.dot(lhs, v[c], preferred_element_type=jnp.float32) for v in (dtheta, dphi))
-        t = t.reshape(groups, 2, 4, 2, radii, halves * 128)
-        d = d.reshape(groups, 2, 4, 2, radii, halves * 128)
-        for g in range(groups):
-            for h in range(halves):
-                here = slice(h * 128, (h + 1) * 128)
-                send[c, g * halves + h] = grid_block(t[g, ..., here], d[g, ..., here])
         if c == 0:
-            pl.semaphore_wait(barrier, greetings)
-        for k in range(n - 1, 0, -1):
-            grid_copy(target(k), me, c).start()
+            load_rest()
+            for g in range(groups):
+                t, d = (
+                    jnp.dot(lhs[g], v[c], preferred_element_type=jnp.float32).reshape(
+                        2, 4, 2, radii, halves * 128
+                    )
+                    for v in (dtheta, dphi)
+                )
+                for h in range(halves):
+                    here = slice(h * 128, (h + 1) * 128)
+                    send[c, g * halves + h] = grid_block(t[..., here], d[..., here])
+                if g == 0:
+                    pl.semaphore_wait(barrier, greetings)
+                for h in range(halves):
+                    e = g * halves + h
+
+                    @pl.when(e != me)
+                    def _(e=e):
+                        grid_copy(e, me, 0).start()
+        else:
+            t, d = (
+                jnp.dot(jnp.concatenate(lhs, axis=0), v[c], preferred_element_type=jnp.float32)
+                for v in (dtheta, dphi)
+            )
+            t = t.reshape(groups, 2, 4, 2, radii, halves * 128)
+            d = d.reshape(groups, 2, 4, 2, radii, halves * 128)
+            for g in range(groups):
+                for h in range(halves):
+                    here = slice(h * 128, (h + 1) * 128)
+                    send[c, g * halves + h] = grid_block(t[g, ..., here], d[g, ..., here])
+            for k in range(n - 1, 0, -1):
+                grid_copy(target(k), me, c).start()
         x[c, me] = send[c, me]
+
+    partner_table(n, pair, partner_rows)
+    table_copy = pltpu.make_async_copy(partner_rows, partner, table_sem.at[0])
+    table_copy.start()
 
     near_first = sorted(range(n), key=lambda e: (e // 4 + e // 2 % 2 + e % 2, -e))
 
@@ -205,7 +233,7 @@
     inverse = 1.0 + half_excess + root
     rho = 1.0 / inverse
     log_rho = -jnp.log(inverse)
-    inner = 1.0 / (2.0 * off * root)
+    inner = alive / (2.0 * off * root)
 
     def power(exponent):
         return jnp.exp(log_rho * exponent)
@@ -243,6 +271,10 @@
     zero = jnp.zeros((radii, 128), jnp.float32)
     for q in range(12):
         states[3 * orders, q] = zero
+    for c in range(chunks):
+        for h in range(halves):
+            piece(2, c, h).wait()
+        turned_table[c] = analysis[c].T
     table_copy.wait()
 
     def chunk_step(c, carry):
@@ -321,33 +353,30 @@
         return carry
 
     lax.fori_loop(0, chunks, chunk_step, 0)
-    for c in range(chunks):
-        for h in range(halves):
-            piece(2, c, h).wait()
-
-    contract = (((1,), (1,)), ((), ()))
 
     def project(c):
         for k in range(1, n):
             e = lax.rem(me + k, n)
             back_copy(e, e, c).wait_recv()
+        terms = []
         for g in range(groups):
             lhs = jnp.concatenate([got[c, g * halves + h] for h in range(halves)], axis=1)
-            total = lax.dot_general(lhs, analysis[c], contract, preferred_element_type=jnp.float32)
+            total = jnp.dot(lhs, turned_table[c], preferred_element_type=jnp.float32)
             total = total.reshape(2, radii, 8, slots)
-            rows = slice(g * radii, (g + 1) * radii)
-            right[rows] += jnp.where(first, total[0], jnp.where(second, total[1], 0.0))
-
-    for c in range(chunks):
-        project(c)
-
-    up = right[0]
-    down = right[points - 1]
+            terms.append(jnp.where(first, total[0], total[1]))
+        return terms
+
+    for c in range(chunks - 1):
+        for g, term in enumerate(project(c)):
+            right[g * radii : (g + 1) * radii] += term
+    terms = project(chunks - 1)
+    source = [right[k] + terms[k // radii][k % radii] for k in range(points)]
+    up, down = source[0], source[points - 1]
     ahead[0] = up
     back[points - 1] = down
     for k in range(1, points):
-        up = right[k] + rho * up
-        down = right[points - 1 - k] + rho * down
+        up = source[k] + rho * up
+        down = source[points - 1 - k] + rho * down
         ahead[k] = up
         back[points - 1 - k] = down
     edges[row] = jnp.concatenate([up, down], axis=0).astype(jnp.bfloat16)
@@ -446,6 +475,7 @@
             table,
             table,
             table,
+            pltpu.VMEM((chunks, halves * 128, slots), jnp.bfloat16),
             pltpu.VMEM((chunks, n, 24 * radii, 128), jnp.bfloat16),
             pltpu.VMEM((chunks, n, 24 * radii, 128), jnp.bfloat16),
             pltpu.VMEM((6 * n + 1, 12, radii, 128), jnp.float32),

time: 35.3 us -> 34.2 us (0.969); the launches traced: 35.2 us -> 33.7 us
  Pallas kernels: 35.2 us -> 33.7 us
    pallas_call x1, Pallas kernels: 34.3 us -> 32.8 us  [local(): pl.pallas_call(functools.partial(step_kernel, n, rows_count), out_shape=(...]
where the time goes in v4:
time: 34.2 us; the launch traced here: 33.7 us
  Pallas kernels  33.7 us (99%)
    pallas_call x1, Pallas kernels, local(): pl.pallas_call(functools.partial(step_kernel, n, rows_count), out_shape=(...  32.8 us
    pallas_call x1, Pallas kernels, local(): pl.pallas_call(finish_kernel, out_shape=jax.ShapeDtypeStruct((8, points,...  0.92 us

profile of v4, /device:TPU:0, one launch (start us, length us, event | category | flops | bytes accessed | tf_op | source)
XLA Modules:
  0.0 33.7 jit_solution(5618853419761157678)
XLA Ops:
  0.0 32.8 %step.1 = (f32[8,32,528]{2,1,0:T(8,128)S(1)}, f32[2,8,528]{2,1,0:T(8,128)S(1)}, f32[4,32,528]{2,1,0:T(8,128)S(1)}, f32[4,32,528]{2,1,0:T(8,128)S(1)}) custom-call(s32[8]{0:T(128)} %pair_hbm.1, f32[4]{0:T(128)} %diffusivity_hbm.1, f32[4,2,32,528]{3,2,1,0:T(8,128)} %spectra_hbm.1, bf16[528,768]{1,0:T(8,128)(2,1)} %dtheta_hbm.1, bf16[528,768]{1,0:T(8,128)(2,1)} %dphi_hbm.1, ...), custom_call_target="tpu_custom_call" | custom-call | tf_op jit(solution)/shard_map/step/pallas_call | solution.py:463
  32.8 0.9 %finish.1 = f32[8,32,528]{2,1,0:T(8,128)} custom-call(f32[8,32,528]{2,1,0:T(8,128)S(1)} %get-tuple-element.9.inside, f32[2,8,528]{2,1,0:T(8,128)S(1)} %get-tuple-element.10.ends, f32[4,32,528]{2,1,0:T(8,128)S(1)} %get-tuple-element.11.rise, f32[4,32,528]{2,1,0:T(8,128)S(1)} %get-tuple-element.12.fall), custom_call_target="tpu_custom_call" | custom-call | tf_op jit(solution)/shard_map/finish/pallas_call | solution.py:507

commit v5 on v4

--- a/solution.py
+++ b/solution.py
@@ -25,16 +25,27 @@
     return first, second, held, degree, order
 
 
-def say_hello(barrier, axis_sizes):
-    total = 0
-    for axis, size in axis_sizes:
-        me = lax.axis_index(axis)
-        for k in range(1, size):
-            pl.semaphore_signal(
-                barrier, inc=1, device_id={axis: lax.rem(me + k, size)}, device_id_type=MESH
-            )
-        total += size - 1
-    return total
+def say_hello(barrier, n, rows_count, me, row):
+    def greet(**device):
+        pl.semaphore_signal(barrier, inc=1, device_id=device, device_id_type=MESH)
+
+    @pl.when(me >= 2)
+    def _():
+        greet(ma=0)
+        greet(ma=1)
+
+    @pl.when(me < 2)
+    def _():
+        for e in range(2, n):
+            greet(ma=e)
+        greet(ma=1 - me)
+
+    @pl.when(me == 0)
+    def _():
+        for k in range(1, rows_count):
+            greet(row=lax.rem(row + k, rows_count))
+
+    return jnp.where(me == 0, n - 1 + rows_count - 1, jnp.where(me == 1, n - 1, 2))
 
 
 def partner_table(n, pair, out):
@@ -65,6 +76,7 @@
     spectra, dtheta, dphi, analysis, turned_table, send, x, states, sums, got, edges, right, ahead, back,
     partner_rows, partner, pair, diffusivity,
     load_sem, piece_sem, table_sem, send_sem, recv_sem, back_send, back_recv, edge_send, edge_recv,
+    plane_sem, planes_sem, rows_sem,
 ):
     me = lax.axis_index("ma")
     row = lax.axis_index("row")
@@ -87,23 +99,33 @@
     loads = [
         pltpu.make_async_copy(source, place, load_sem.at[i])
         for i, (source, place) in enumerate(
-            [(pair_hbm, pair), (spectra_hbm, spectra), (diffusivity_hbm, diffusivity)]
+            [(pair_hbm, pair), (diffusivity_hbm, diffusivity)]
+            + [
+                (
+                    spectra_hbm.at[:, :, g * radii : (g + 1) * radii],
+                    spectra.at[:, :, g * radii : (g + 1) * radii],
+                )
+                for g in range(groups)
+            ]
         )
     ]
-    barrier = pltpu.get_barrier_semaphore()
-    greetings = say_hello(barrier, [("ma", n), ("row", rows_count)])
     loads[0].start()
-    loads[1].start()
+    loads[2].start()
     for h in range(halves):
         piece(0, 0, h).start()
         piece(1, 0, h).start()
+    for g in range(1, groups):
+        loads[2 + g].start()
+
+    barrier = pltpu.get_barrier_semaphore()
+    greetings = say_hello(barrier, n, rows_count, me, row)
 
     def load_rest():
         for i in range(2):
             for c in range(1, chunks):
                 for h in range(halves):
                     piece(i, c, h).start()
-        loads[2].start()
+        loads[1].start()
         for c in range(chunks):
             for h in range(halves):
                 piece(2, c, h).start()
@@ -114,12 +136,12 @@
     lowest = pair[me]
     first, second, held, degree, order = slot_rows(lowest, slots)
 
-    loads[1].wait()
-    lhs = []
-    for g in range(groups):
+    def group_rows(g):
         v = spectra[:, :, g * radii : (g + 1) * radii, :].reshape(8 * radii, slots)
         v = jnp.concatenate([jnp.where(first, v, 0.0), jnp.where(second, v, 0.0)], axis=0)
-        lhs.append(v.astype(jnp.bfloat16))
+        return v.astype(jnp.bfloat16)
+
+    lhs = []
 
     def grid_block(t, d):
         parts = []
@@ -152,6 +174,9 @@
             device_id={"ma": e}, device_id_type=MESH,
         )
 
+    def tell(sem, **device):
+        pl.semaphore_signal(sem, inc=1, device_id=device, device_id_type=MESH)
+
     tall = n // 4
     my_y, my_x, my_core = me // 4, lax.rem(me // 2, 2), lax.rem(me, 2)
 
@@ -168,6 +193,8 @@
         if c == 0:
             load_rest()
             for g in range(groups):
+                loads[2 + g].wait()
+                lhs.append(group_rows(g))
                 t, d = (
                     jnp.dot(lhs[g], v[c], preferred_element_type=jnp.float32).reshape(
                         2, 4, 2, radii, halves * 128
@@ -179,8 +206,22 @@
                     send[c, g * halves + h] = grid_block(t[..., here], d[..., here])
                 if g == 0:
                     pl.semaphore_wait(barrier, greetings)
+
+                    @pl.when(me == 0)
+                    def _():
+                        for e in range(2, n):
+                            tell(plane_sem, ma=e)
+                        for k in range(1, rows_count):
+                            tell(planes_sem, row=lax.rem(row + k, rows_count))
+
                 for h in range(halves):
                     e = g * halves + h
+                    if e == 2:
+
+                        @pl.when(me >= 2)
+                        def _():
+                            pl.semaphore_wait(plane_sem, 1)
+
 
                     @pl.when(e != me)
                     def _(e=e):
@@ -196,13 +237,19 @@
                 for h in range(halves):
                     here = slice(h * 128, (h + 1) * 128)
                     send[c, g * halves + h] = grid_block(t[g, ..., here], d[g, ..., here])
-            for k in range(n - 1, 0, -1):
-                grid_copy(target(k), me, c).start()
-        x[c, me] = send[c, me]
+            for e in range(n):
+
+                @pl.when(e != me)
+                def _(e=e, c=c):
+                    grid_copy(e, me, c).start()
+
 
     partner_table(n, pair, partner_rows)
     table_copy = pltpu.make_async_copy(partner_rows, partner, table_sem.at[0])
     table_copy.start()
+
+    for c in range(chunks):
+        x[c, me] = send[c, me]
 
     near_first = sorted(range(n), key=lambda e: (e // 4 + e // 2 % 2 + e % 2, -e))
 
@@ -221,7 +268,7 @@
     upper = jnp.where(degree < LMAX, upper * alive, 0.0) * ROTATION
     spin = ROTATION * m / (l * (l + 1.0) + 2.0) * alive
 
-    loads[2].wait()
+    loads[1].wait()
     all_points = points * rows_count
     field = lax.broadcasted_iota(jnp.int32, (8, 1), 0) // 2
     nu = jnp.zeros((8, 1), jnp.float32)
@@ -277,6 +324,12 @@
         turned_table[c] = analysis[c].T
     table_copy.wait()
 
+    @pl.when(me == 0)
+    def _():
+        pl.semaphore_wait(planes_sem, rows_count - 1)
+        for e in range(1, n):
+            tell(rows_sem, ma=e)
+
     def chunk_step(c, carry):
         def unpack(k, carry):
             g = target(k)
@@ -379,6 +432,10 @@
         down = source[points - 1 - k] + rho * down
         ahead[k] = up
         back[points - 1 - k] = down
+    @pl.when(me > 0)
+    def _():
+        pl.semaphore_wait(rows_sem, 1)
+
     edges[row] = jnp.concatenate([up, down], axis=0).astype(jnp.bfloat16)
 
     def edge_copy(e, source):
@@ -489,7 +546,7 @@
             pltpu.SMEM((2 * n, 128), jnp.int32),
             pltpu.SMEM(pair_index.shape, jnp.int32),
             pltpu.SMEM(diffusivity.shape, jnp.float32),
-            pltpu.SemaphoreType.DMA((3,)),
+            pltpu.SemaphoreType.DMA((2 + points // radii,)),
             pltpu.SemaphoreType.DMA((3, chunks, halves)),
             pltpu.SemaphoreType.DMA((1,)),
             pltpu.SemaphoreType.DMA((chunks, n)),
@@ -498,6 +555,9 @@
             pltpu.SemaphoreType.DMA((chunks, n)),
             pltpu.SemaphoreType.DMA((rows_count,)),
             pltpu.SemaphoreType.DMA((rows_count,)),
+            pltpu.SemaphoreType.REGULAR,
+            pltpu.SemaphoreType.REGULAR,
+            pltpu.SemaphoreType.REGULAR,
         ],
         compiler_params=pltpu.CompilerParams(
             collective_id=0, has_side_effects=True, vmem_limit_bytes=VMEM_LIMIT

time: 34.2 us -> 34 us (level)
  Pallas kernels: 33.7 us -> 33.3 us
    pallas_call x1, Pallas kernels: 32.8 us -> 32.4 us  [local(): pl.pallas_call(functools.partial(step_kernel, n, rows_count), out_shape=(...]
where the time goes in v5:
time: 34 us; the launch traced here: 33.3 us
  Pallas kernels  33.3 us (98%)
    pallas_call x1, Pallas kernels, local(): pl.pallas_call(functools.partial(step_kernel, n, rows_count), out_shape=(...  32.4 us
    pallas_call x1, Pallas kernels, local(): pl.pallas_call(finish_kernel, out_shape=jax.ShapeDtypeStruct((8, points,...  0.92 us

profile of v5, /device:TPU:0, one launch (start us, length us, event | category | flops | bytes accessed | tf_op | source)
XLA Modules:
  0.0 33.3 jit_solution(8171832378479344062)
XLA Ops:
  0.0 32.4 %step.1 = (f32[8,32,528]{2,1,0:T(8,128)S(1)}, f32[2,8,528]{2,1,0:T(8,128)S(1)}, f32[4,32,528]{2,1,0:T(8,128)S(1)}, f32[4,32,528]{2,1,0:T(8,128)S(1)}) custom-call(s32[8]{0:T(128)} %pair_hbm.1, f32[4]{0:T(128)} %diffusivity_hbm.1, f32[4,2,32,528]{3,2,1,0:T(8,128)} %spectra_hbm.1, bf16[528,768]{1,0:T(8,128)(2,1)} %dtheta_hbm.1, bf16[528,768]{1,0:T(8,128)(2,1)} %dphi_hbm.1, ...), custom_call_target="tpu_custom_call" | custom-call | tf_op jit(solution)/shard_map/step/pallas_call | solution.py:520
  32.4 0.9 %finish.1 = f32[8,32,528]{2,1,0:T(8,128)} custom-call(f32[8,32,528]{2,1,0:T(8,128)S(1)} %get-tuple-element.9.inside, f32[2,8,528]{2,1,0:T(8,128)S(1)} %get-tuple-element.10.ends, f32[4,32,528]{2,1,0:T(8,128)S(1)} %get-tuple-element.11.rise, f32[4,32,528]{2,1,0:T(8,128)S(1)} %get-tuple-element.12.fall), custom_call_target="tpu_custom_call" | custom-call | tf_op jit(solution)/shard_map/finish/pallas_call | solution.py:567

commit v6 on v5

--- a/solution.py
+++ b/solution.py
@@ -419,9 +419,20 @@
             terms.append(jnp.where(first, total[0], total[1]))
         return terms
 
-    for c in range(chunks - 1):
-        for g, term in enumerate(project(c)):
-            right[g * radii : (g + 1) * radii] += term
+    early = chunks - 1
+    if early:
+        for c in range(early):
+            for k in range(1, n):
+                e = lax.rem(me + k, n)
+                back_copy(e, e, c).wait_recv()
+        table = turned_table[0:early].reshape(early * halves * 128, slots)
+        for g in range(groups):
+            lhs = jnp.concatenate(
+                [got[c, g * halves + h] for c in range(early) for h in range(halves)], axis=1
+            )
+            total = jnp.dot(lhs, table, preferred_element_type=jnp.float32)
+            total = total.reshape(2, radii, 8, slots)
+            right[g * radii : (g + 1) * radii] += jnp.where(first, total[0], total[1])
     terms = project(chunks - 1)
     source = [right[k] + terms[k // radii][k % radii] for k in range(points)]
     up, down = source[0], source[points - 1]

time: 34 us -> 34 us (level)
  no operation moved by 1% of the time
where the time goes in v6:
time: 34 us; the launch traced here: 33.3 us
  Pallas kernels  33.3 us (98%)
    pallas_call x1, Pallas kernels, local(): pl.pallas_call(functools.partial(step_kernel, n, rows_count), out_shape=(...  32.4 us
    pallas_call x1, Pallas kernels, local(): pl.pallas_call(finish_kernel, out_shape=jax.ShapeDtypeStruct((8, points,...  0.92 us

profile of v6, /device:TPU:0, one launch (start us, length us, event | category | flops | bytes accessed | tf_op | source)
XLA Modules:
  0.0 33.3 jit_solution(16821793145489710274)
XLA Ops:
  0.0 32.4 %step.1 = (f32[8,32,528]{2,1,0:T(8,128)S(1)}, f32[2,8,528]{2,1,0:T(8,128)S(1)}, f32[4,32,528]{2,1,0:T(8,128)S(1)}, f32[4,32,528]{2,1,0:T(8,128)S(1)}) custom-call(s32[8]{0:T(128)} %pair_hbm.1, f32[4]{0:T(128)} %diffusivity_hbm.1, f32[4,2,32,528]{3,2,1,0:T(8,128)} %spectra_hbm.1, bf16[528,768]{1,0:T(8,128)(2,1)} %dtheta_hbm.1, bf16[528,768]{1,0:T(8,128)(2,1)} %dphi_hbm.1, ...), custom_call_target="tpu_custom_call" | custom-call | tf_op jit(solution)/shard_map/step/pallas_call | solution.py:531
  32.4 0.9 %finish.1 = f32[8,32,528]{2,1,0:T(8,128)} custom-call(f32[8,32,528]{2,1,0:T(8,128)S(1)} %get-tuple-element.9.inside, f32[2,8,528]{2,1,0:T(8,128)S(1)} %get-tuple-element.10.ends, f32[4,32,528]{2,1,0:T(8,128)S(1)} %get-tuple-element.11.rise, f32[4,32,528]{2,1,0:T(8,128)S(1)} %get-tuple-element.12.fall), custom_call_target="tpu_custom_call" | custom-call | tf_op jit(solution)/shard_map/finish/pallas_call | solution.py:578
